TPU v7x, 256 devices: a whole 4x4x8 slice. The times are simulated.
256 devices in a mesh: row: 16 (over z, x_hi), col: 16 (over x_lo, y, core).
Axes of the slice: x: 4 (x_hi: 2, x_lo: 2; x = x_hi * 2 + x_lo), y: 4, z: 8, core: 2. Of those that a mesh axis runs over, the one named last changes fastest.
Arguments:
- sensitivity: bfloat16 [16, 16, 8, 96, 256], P('row', 'col'), may hold values from -0.41992188 to 0.41992188
- block_ids: int32 [16, 16, 8], replicated, may hold values from 0 to 63, as said below
- covariance: float32 [64, 256], replicated, may hold values from 0.05 to 1
Outputs:
- gram: float32 [16, 1536, 16, 1536], P('row', None, 'col')
Inputs may be any that keep to these rules, and one draw needn't show every extreme that they name: `block_ids`: the 8 ids of one station group at one period are distinct; footprints widen with the period index.
All inputs are finite; a program needn't handle non-finite values.
Results may differ from a plain program's by a relative error of at most 0.0024.
Values may be sent and summed in bfloat16 or wider, within the bound.
A program may use at most 128 MiB of HBM per device.

v0:
```python
import jax
import jax.numpy as jnp
from jax import lax
from jax.sharding import PartitionSpec as P


def tile_columns(rows, row_ids, cols, col_ids):

    def one_row(args):
        block, ids = args
        match = (ids[None, :, None] == col_ids[:, None, :]).astype(jnp.bfloat16)
        aligned = jnp.einsum(
            "akl,alje->akje", match, cols, preferred_element_type=jnp.float32
        ).astype(jnp.bfloat16)
        return jnp.einsum("kie,akje->iaj", block, aligned, preferred_element_type=jnp.float32)

    result = lax.map(one_row, (rows, row_ids))
    return result.reshape(rows.shape[0] * rows.shape[2], cols.shape[0] * cols.shape[2])


def body(sensitivity, block_ids, covariance):
    row_index = lax.axis_index("row")
    col_index = lax.axis_index("col")
    row_ids = lax.dynamic_index_in_dim(block_ids, row_index, 0, keepdims=False)
    col_ids = lax.dynamic_index_in_dim(block_ids, col_index, 1, keepdims=False)
    own_ids = lax.dynamic_index_in_dim(row_ids, col_index, 0, keepdims=False)
    blocks_total = covariance.shape[0]
    onehot = (own_ids[:, None] == jnp.arange(blocks_total, dtype=jnp.int32)[None, :]).astype(
        jnp.float32
    )
    factors = jnp.dot(onehot, covariance, precision=lax.Precision.HIGHEST)
    scaled = (sensitivity.astype(jnp.float32) * factors[None, None, :, None, :]).astype(
        jnp.bfloat16
    )
    rows = lax.all_gather(scaled, "col", axis=1, tiled=True)[0]
    cols = lax.all_gather(sensitivity, "row", axis=0, tiled=True)[:, 0]
    tile = tile_columns(rows, row_ids, cols, col_ids)
    return tile.reshape(1, tile.shape[0], 1, tile.shape[1])


def solution(mesh):
    placed = (P("row", "col", None, None, None), P(), P())
    return jax.shard_map(
        body, mesh=mesh, in_specs=placed, out_specs=P("row", None, "col", None), check_vma=False
    )
```

profile of v0, /device:TPU:1, one launch (start us, length us, event | category | flops | bytes accessed | tf_op | source)
XLA Modules:
  0.0 349.1 jit_solution(1650555240496740621)
XLA Ops:
  6.5 0.0 copy-start
  6.5 0.7 all-gather.5.cloned.1.call-update
  7.3 0.0 all-gather.3.cloned.1.call-start
  7.3 0.9 dynamic-slice_reduce_fusion
  8.2 0.2 fusion.13
  8.4 1.9 multiply_convert_fusion
  10.3 0.0 all-gather.3.cloned.1.call-update
  10.3 0.9 constant_dynamic-slice_fusion.1
  11.2 0.2 copy.26
  11.4 0.7 dynamic-slice_bitcast_fusion
  12.1 0.1 copy.17
  12.2 116.5 %all-gather.5.cloned.1.call-done = bf16[16,1,8,96,256]{4,3,2,1,0:T(8,128)(2,1)} async-done(((bf16[1,1,8,96,256]{4,3,2,1,0:T(8,128)(2,1)}), bf16[16,1,8,96,256]{4,3,2,1,0:T(8,128)(2,1)}) %all-gather.5.cloned.1.call-update) | async-done | bytes 6291472 | tf_op jit(solution)/shard_map/all_gather | solution.py:36
  128.7 9.8 %copy.19 = bf16[16,8,96,256]{3,1,2,0:T(8,128)(2,1)} copy(bf16[16,8,96,256]{3,2,1,0:T(8,128)(2,1)} %bitcast.37) | data formatting | bytes 12582912 | tf_op jit(solution)/shard_map/while | solution.py:17
  138.5 35.2 %all-gather.3.cloned.1.call-done = bf16[1,16,8,96,256]{4,3,2,0,1:T(8,128)(2,1)} async-done(((bf16[1,1,8,96,256]{4,3,2,0,1:T(8,128)(2,1)}), bf16[1,16,8,96,256]{4,3,2,0,1:T(8,128)(2,1)}) %all-gather.3.cloned.1.call-update) | async-done | bytes 6291472 | tf_op jit(solution)/shard_map/all_gather | solution.py:35
  173.6 151.4 %while.10 = (s32[]{:T(128)}, f32[16,96,16,96]{3,2,1,0:T(8,128)}, bf16[16,8,96,256]{3,2,1,0:T(8,128)(2,1)}, s32[16,8]{1,0:T(8,128)S(1)}, s32[16,8]{1,0:T(8,128)S(1)}, /*index=5*/bf16[16,8,96,256]{3,1,2,0:T(8,128)(2,1)}, s32[]{:T(128)}) while((s32[]{:T(128)}, f32[16,96,16,96]{3,2,1,0:T(8,128)}, bf16[16,8,96,256]{3,2,1,0:T(8,128)(2,1)}, ...), condition=%wide.region_1.2_spmd, body=%wide.region_0.1_spmd.sunk | while | flops 657458176 | bytes 21235376 | solution.py:17
  173.6 4.6 %convolution_convert_fusion.2 = bf16[16,8,96,256]{3,1,2,0:T(8,128)(2,1)S(1)} fusion(bf16[16,8,96,256]{3,1,2,0:T(8,128)(2,1)} %get-tuple-element.124, s32[16,8]{1,0:T(8,128)S(1)} %get-tuple-element.123, s32[8]{0:T(128)S(1)} %fusion.27), kind=kOutput, calls=%fused_computation.2.clone.1 | convolution fusion | flops 53478400 | bytes 12583456 | tf_op jit(solution)/shard_map/while/body/eval_jaxpr/akl,alje->akje/dot_general | solution.py:12
  178.3 3.5 fusion.28
  181.7 1.4 copy_dynamic-update-slice_fusion.2
  183.1 4.6 %convolution_convert_fusion.2 = bf16[16,8,96,256]{3,1,2,0:T(8,128)(2,1)S(1)} fusion(bf16[16,8,96,256]{3,1,2,0:T(8,128)(2,1)} %get-tuple-element.124, s32[16,8]{1,0:T(8,128)S(1)} %get-tuple-element.123, s32[8]{0:T(128)S(1)} %fusion.27), kind=kOutput, calls=%fused_computation.2.clone.1 | convolution fusion | flops 53478400 | bytes 12583456 | tf_op jit(solution)/shard_map/while/body/eval_jaxpr/akl,alje->akje/dot_general | solution.py:12
  187.7 3.5 fusion.28
  191.2 1.4 copy_dynamic-update-slice_fusion.2
  192.6 4.6 %convolution_convert_fusion.2 = bf16[16,8,96,256]{3,1,2,0:T(8,128)(2,1)S(1)} fusion(bf16[16,8,96,256]{3,1,2,0:T(8,128)(2,1)} %get-tuple-element.124, s32[16,8]{1,0:T(8,128)S(1)} %get-tuple-element.123, s32[8]{0:T(128)S(1)} %fusion.27), kind=kOutput, calls=%fused_computation.2.clone.1 | convolution fusion | flops 53478400 | bytes 12583456 | tf_op jit(solution)/shard_map/while/body/eval_jaxpr/akl,alje->akje/dot_general | solution.py:12
  197.2 3.5 fusion.28
  200.7 1.4 copy_dynamic-update-slice_fusion.2
  202.0 4.6 %convolution_convert_fusion.2 = bf16[16,8,96,256]{3,1,2,0:T(8,128)(2,1)S(1)} fusion(bf16[16,8,96,256]{3,1,2,0:T(8,128)(2,1)} %get-tuple-element.124, s32[16,8]{1,0:T(8,128)S(1)} %get-tuple-element.123, s32[8]{0:T(128)S(1)} %fusion.27), kind=kOutput, calls=%fused_computation.2.clone.1 | convolution fusion | flops 53478400 | bytes 12583456 | tf_op jit(solution)/shard_map/while/body/eval_jaxpr/akl,alje->akje/dot_general | solution.py:12
  206.6 3.5 fusion.28
  210.1 1.3 copy_dynamic-update-slice_fusion.2
  211.5 4.6 %convolution_convert_fusion.2 = bf16[16,8,96,256]{3,1,2,0:T(8,128)(2,1)S(1)} fusion(bf16[16,8,96,256]{3,1,2,0:T(8,128)(2,1)} %get-tuple-element.124, s32[16,8]{1,0:T(8,128)S(1)} %get-tuple-element.123, s32[8]{0:T(128)S(1)} %fusion.27), kind=kOutput, calls=%fused_computation.2.clone.1 | convolution fusion | flops 53478400 | bytes 12583456 | tf_op jit(solution)/shard_map/while/body/eval_jaxpr/akl,alje->akje/dot_general | solution.py:12
  216.1 3.5 fusion.28
  219.6 1.3 copy_dynamic-update-slice_fusion.2
  220.9 4.6 %convolution_convert_fusion.2 = bf16[16,8,96,256]{3,1,2,0:T(8,128)(2,1)S(1)} fusion(bf16[16,8,96,256]{3,1,2,0:T(8,128)(2,1)} %get-tuple-element.124, s32[16,8]{1,0:T(8,128)S(1)} %get-tuple-element.123, s32[8]{0:T(128)S(1)} %fusion.27), kind=kOutput, calls=%fused_computation.2.clone.1 | convolution fusion | flops 53478400 | bytes 12583456 | tf_op jit(solution)/shard_map/while/body/eval_jaxpr/akl,alje->akje/dot_general | solution.py:12
  225.5 3.5 fusion.28
  229.0 1.4 copy_dynamic-update-slice_fusion.2
  230.4 4.6 %convolution_convert_fusion.2 = bf16[16,8,96,256]{3,1,2,0:T(8,128)(2,1)S(1)} fusion(bf16[16,8,96,256]{3,1,2,0:T(8,128)(2,1)} %get-tuple-element.124, s32[16,8]{1,0:T(8,128)S(1)} %get-tuple-element.123, s32[8]{0:T(128)S(1)} %fusion.27), kind=kOutput, calls=%fused_computation.2.clone.1 | convolution fusion | flops 53478400 | bytes 12583456 | tf_op jit(solution)/shard_map/while/body/eval_jaxpr/akl,alje->akje/dot_general | solution.py:12
  235.0 3.5 fusion.28
  238.5 1.4 copy_dynamic-update-slice_fusion.2
  239.8 4.6 %convolution_convert_fusion.2 = bf16[16,8,96,256]{3,1,2,0:T(8,128)(2,1)S(1)} fusion(bf16[16,8,96,256]{3,1,2,0:T(8,128)(2,1)} %get-tuple-element.124, s32[16,8]{1,0:T(8,128)S(1)} %get-tuple-element.123, s32[8]{0:T(128)S(1)} %fusion.27), kind=kOutput, calls=%fused_computation.2.clone.1 | convolution fusion | flops 53478400 | bytes 12583456 | tf_op jit(solution)/shard_map/while/body/eval_jaxpr/akl,alje->akje/dot_general | solution.py:12
  244.5 3.5 fusion.28
  247.9 1.4 copy_dynamic-update-slice_fusion.2
  249.3 4.6 %convolution_convert_fusion.2 = bf16[16,8,96,256]{3,1,2,0:T(8,128)(2,1)S(1)} fusion(bf16[16,8,96,256]{3,1,2,0:T(8,128)(2,1)} %get-tuple-element.124, s32[16,8]{1,0:T(8,128)S(1)} %get-tuple-element.123, s32[8]{0:T(128)S(1)} %fusion.27), kind=kOutput, calls=%fused_computation.2.clone.1 | convolution fusion | flops 53478400 | bytes 12583456 | tf_op jit(solution)/shard_map/while/body/eval_jaxpr/akl,alje->akje/dot_general | solution.py:12
  253.9 3.5 fusion.28
  257.4 1.3 copy_dynamic-update-slice_fusion.2
  258.7 4.6 %convolution_convert_fusion.2 = bf16[16,8,96,256]{3,1,2,0:T(8,128)(2,1)S(1)} fusion(bf16[16,8,96,256]{3,1,2,0:T(8,128)(2,1)} %get-tuple-element.124, s32[16,8]{1,0:T(8,128)S(1)} %get-tuple-element.123, s32[8]{0:T(128)S(1)} %fusion.27), kind=kOutput, calls=%fused_computation.2.clone.1 | convolution fusion | flops 53478400 | bytes 12583456 | tf_op jit(solution)/shard_map/while/body/eval_jaxpr/akl,alje->akje/dot_general | solution.py:12
  263.4 3.5 fusion.28
  266.8 1.3 copy_dynamic-update-slice_fusion.2
  268.2 4.6 %convolution_convert_fusion.2 = bf16[16,8,96,256]{3,1,2,0:T(8,128)(2,1)S(1)} fusion(bf16[16,8,96,256]{3,1,2,0:T(8,128)(2,1)} %get-tuple-element.124, s32[16,8]{1,0:T(8,128)S(1)} %get-tuple-element.123, s32[8]{0:T(128)S(1)} %fusion.27), kind=kOutput, calls=%fused_computation.2.clone.1 | convolution fusion | flops 53478400 | bytes 12583456 | tf_op jit(solution)/shard_map/while/body/eval_jaxpr/akl,alje->akje/dot_general | solution.py:12
  272.8 3.5 fusion.28
  276.2 1.4 copy_dynamic-update-slice_fusion.2
  277.7 4.6 %convolution_convert_fusion.2 = bf16[16,8,96,256]{3,1,2,0:T(8,128)(2,1)S(1)} fusion(bf16[16,8,96,256]{3,1,2,0:T(8,128)(2,1)} %get-tuple-element.124, s32[16,8]{1,0:T(8,128)S(1)} %get-tuple-element.123, s32[8]{0:T(128)S(1)} %fusion.27), kind=kOutput, calls=%fused_computation.2.clone.1 | convolution fusion | flops 53478400 | bytes 12583456 | tf_op jit(solution)/shard_map/while/body/eval_jaxpr/akl,alje->akje/dot_general | solution.py:12
  282.3 3.5 fusion.28
  285.8 1.4 copy_dynamic-update-slice_fusion.2
  287.2 4.6 %convolution_convert_fusion.2 = bf16[16,8,96,256]{3,1,2,0:T(8,128)(2,1)S(1)} fusion(bf16[16,8,96,256]{3,1,2,0:T(8,128)(2,1)} %get-tuple-element.124, s32[16,8]{1,0:T(8,128)S(1)} %get-tuple-element.123, s32[8]{0:T(128)S(1)} %fusion.27), kind=kOutput, calls=%fused_computation.2.clone.1 | convolution fusion | flops 53478400 | bytes 12583456 | tf_op jit(solution)/shard_map/while/body/eval_jaxpr/akl,alje->akje/dot_general | solution.py:12
  291.8 3.5 fusion.28
  295.3 1.3 copy_dynamic-update-slice_fusion.2
  296.6 4.6 %convolution_convert_fusion.2 = bf16[16,8,96,256]{3,1,2,0:T(8,128)(2,1)S(1)} fusion(bf16[16,8,96,256]{3,1,2,0:T(8,128)(2,1)} %get-tuple-element.124, s32[16,8]{1,0:T(8,128)S(1)} %get-tuple-element.123, s32[8]{0:T(128)S(1)} %fusion.27), kind=kOutput, calls=%fused_computation.2.clone.1 | convolution fusion | flops 53478400 | bytes 12583456 | tf_op jit(solution)/shard_map/while/body/eval_jaxpr/akl,alje->akje/dot_general | solution.py:12
  301.3 3.5 fusion.28
  304.7 1.4 copy_dynamic-update-slice_fusion.2
  306.1 4.6 %convolution_convert_fusion.2 = bf16[16,8,96,256]{3,1,2,0:T(8,128)(2,1)S(1)} fusion(bf16[16,8,96,256]{3,1,2,0:T(8,128)(2,1)} %get-tuple-element.124, s32[16,8]{1,0:T(8,128)S(1)} %get-tuple-element.123, s32[8]{0:T(128)S(1)} %fusion.27), kind=kOutput, calls=%fused_computation.2.clone.1 | convolution fusion | flops 53478400 | bytes 12583456 | tf_op jit(solution)/shard_map/while/body/eval_jaxpr/akl,alje->akje/dot_general | solution.py:12
  310.7 3.5 fusion.28
  314.2 1.3 copy_dynamic-update-slice_fusion.2
  315.6 4.6 %convolution_convert_fusion.2 = bf16[16,8,96,256]{3,1,2,0:T(8,128)(2,1)S(1)} fusion(bf16[16,8,96,256]{3,1,2,0:T(8,128)(2,1)} %get-tuple-element.124, s32[16,8]{1,0:T(8,128)S(1)} %get-tuple-element.123, s32[8]{0:T(128)S(1)} %fusion.27), kind=kOutput, calls=%fused_computation.2.clone.1 | convolution fusion | flops 53478400 | bytes 12583456 | tf_op jit(solution)/shard_map/while/body/eval_jaxpr/akl,alje->akje/dot_general | solution.py:12
  320.2 3.5 fusion.28
  323.7 1.4 copy_dynamic-update-slice_fusion.2
  325.0 17.2 %reshape_reshape.3 = f32[1,1536,1,1536]{3,2,1,0:T(1,128)} reshape(f32[16,96,16,96]{3,2,1,0:T(8,128)} %get-tuple-element.37) | data formatting | bytes 18874368 | tf_op jit(solution)/shard_map/reshape;reshape | solution.py:38
  (19 shorter events, 0.1 us)
Async XLA Ops:
  6.5 1.7 copy-start
  6.5 122.2 %all-gather.5.cloned.1.call-start = ((), (), s32[]{:S(2)}) async-start(), calls=%async_computation.1 | async-start | bytes 6684672 | tf_op jit(solution)/shard_map/all_gather | solution.py:36
  7.3 166.4 %all-gather.3.cloned.1.call-start = ((), (), s32[]{:S(2)}) async-start(), calls=%async_computation | async-start | bytes 6684672 | tf_op jit(solution)/shard_map/all_gather | solution.py:35
Sparse Core Ops, SparseCore 0:
  9.9 118.7 all-gather.4
  130.5 43.0 all-gather.2
where the time goes:
time: 351 us; the launch traced here: 349 us
  waiting for transfers between devices  152 us (43%)
  matrix products  129 us (37%)
  local copies, waits for them, and re-layouts  51.6 us (15%)
  between operations  13.4 us (4%)
    all_gather x1, waiting for transfers between devices, body(): cols = lax.all_gather(sensitivity, 'row', axis=0, tiled=True)[:, 0]  117 us
    dot_general x16, matrix products, one_row(): jnp.einsum('akl,alje->akje', match, cols, preferred_element_type=jnp.floa...  74 us
    dot_general x16, matrix products, one_row(): jnp.einsum('kie,akje->iaj', block, aligned, preferred_element_type=jnp.fl...  55.3 us
    all_gather x1, waiting for transfers between devices, body(): rows = lax.all_gather(scaled, 'col', axis=1, tiled=True)[0]  35.2 us
    dynamic_update_slice x16, local copies, waits for them, and re-layouts, tile_columns(): result = lax.map(one_row, (rows, row_ids))  21.8 us
    another operation x1, local copies, waits for them, and re-layouts, body(): return tile.reshape(1, tile.shape[0], 1, tile.shape[1])  17.2 us
    while x2, local copies, waits for them, and re-layouts, tile_columns(): result = lax.map(one_row, (rows, row_ids))  9.84 us
  transfers between devices with their start and end apart: 2, of which 2 were waited for; matrix products, arithmetic and copies ran while one was open for 4% of the time, Pallas kernels for 0%

commit v1 on v0

v1 whole, which is shorter than its diff:
```python
import functools
import jax
import jax.numpy as jnp
from jax import lax
from jax.experimental import pallas as pl
from jax.experimental.pallas import tpu as pltpu
from jax.sharding import PartitionSpec as P

MESH = pl.DeviceIdType.MESH
NX, NY, NZ = 4, 4, 8


def gather_kernel(chunk, ids_ref, sens_ref, cov_ref, cols_ref, rows_ref, own, scaled, local_sem, send_sem, recv_sem):
    row = lax.axis_index("row")
    col = lax.axis_index("col")
    z, x_hi = row // 2, row % 2
    x_lo, y, core = col // 8, (col // 2) % 4, col % 2
    blocks = sens_ref.shape[0]
    half = blocks // 2

    def station(z_at, x_hi_at):
        return ((z_at + NZ) % NZ) * 2 + x_hi_at

    def period(x_lo_at, y_at, core_at):
        return (x_lo_at * NY + (y_at + NY) % NY) * 2 + core_at

    z_dev = {d: (station(z + d, x_hi), col) for d in (1, -1)}
    y_dev = {d: (row, period(x_lo, y + d, core)) for d in (1, -1)}
    far_dev = (station(z, 1 - x_hi), col)
    side_dev = (row, period(1 - x_lo, y, core))
    twin_dev = (row, period(x_lo, y, 1 - core))

    load = pltpu.make_async_copy(sens_ref, own, local_sem.at[0])
    load.start()
    keep = pltpu.make_async_copy(sens_ref, cols_ref.at[row], local_sem.at[1])
    keep.start()

    barrier = pltpu.get_barrier_semaphore()
    partners = [z_dev[1], z_dev[-1], y_dev[1], y_dev[-1], far_dev, side_dev, twin_dev]
    for device in partners:
        pl.semaphore_signal(barrier, inc=1, device_id=device, device_id_type=MESH)
    pl.semaphore_wait(barrier, len(partners))

    copies = {}

    def send(key, src, dst, device):
        n = len(copies)
        copy = pltpu.make_async_remote_copy(
            src_ref=src, dst_ref=dst, send_sem=send_sem.at[n], recv_sem=recv_sem.at[n], device_id=device, device_id_type=MESH
        )
        copy.start()
        copies[key] = copy

    def z_blocks(name, d, step):
        first, size = streams[name]
        if step == 4:
            return (first, size // 2) if d == 1 else (first + size // 2, size // 2)
        return first, size

    streams = {}
    names = {"b": [], "a": [], "p": []}
    for kind, base in (("b", half), ("a", 0), ("p", 0)):
        for first in range(base, base + half, chunk):
            streams[(kind, first)] = (first, chunk)
            names[kind].append((kind, first))

    def send_z(name, d, step):
        first, size = z_blocks(name, d, step)
        slot = station(z - d * (step - 1), 1 - x_hi if name[0] == "p" else x_hi)
        src = sens_ref if (step == 1 and name[0] != "p") else cols_ref.at[slot]
        send(("z", name, d, step), src.at[pl.ds(first, size)], cols_ref.at[slot, pl.ds(first, size)], z_dev[d])

    def send_far(name, d, step):
        first, size = z_blocks(name, d, step)
        slot = station(z - d * step, x_hi)
        src = sens_ref if step == 0 else cols_ref.at[slot]
        send(("far", name, d, step), src.at[pl.ds(first, size)], cols_ref.at[slot, pl.ds(first, size)], far_dev)

    def take_z(name, d, step):
        copies[("z", name, d, step)].wait_recv()
        if step < 4:
            send_z(name, d, step + 1)
        if name[0] == "b":
            send_far(name, d, step)

    for name in names["b"]:
        for d in (1, -1):
            send_z(name, d, 1)
    for name in names["b"]:
        send_far(name, 1, 0)
    for name in names["a"]:
        for d in (1, -1):
            send_z(name, d, 1)

    load.wait()
    for k in range(blocks):
        factor = cov_ref[pl.ds(ids_ref[(row * 16 + col) * blocks + k], 1), :]
        scaled[k] = (own[k].astype(jnp.float32) * factor).astype(jnp.bfloat16)
    keep_row = pltpu.make_async_copy(scaled, rows_ref.at[col], local_sem.at[2])
    keep_row.start()
    send(("side",), scaled, rows_ref.at[col], side_dev)
    for d in (1, -1):
        send(("y", 0, d), scaled, rows_ref.at[col], y_dev[d])
    send(("twin", "own"), scaled, rows_ref.at[col], twin_dev)
    for name in names["a"]:
        send_far(name, 1, 0)

    def twin(key, slot, first, size):
        ref = rows_ref.at[slot, pl.ds(first, size)]
        send(("twin", key), ref, ref, twin_dev)

    def take_y(line, d):
        copies[("y", line, d)].wait_recv()
        slot = period(x_lo if line == 0 else 1 - x_lo, y - d, core)
        first = 0 if d == 1 else half
        ref = rows_ref.at[slot, pl.ds(first, half)]
        send(("y2", line, d), ref, ref, y_dev[d])
        twin(("y", line, d), slot, 0, blocks)

    def take_y2(line, d):
        copies[("y2", line, d)].wait_recv()
        slot = period(x_lo if line == 0 else 1 - x_lo, y - 2 * d, core)
        twin(("y2", line, d), slot, 0 if d == 1 else half, half)

    def z_round(kinds, step):
        for kind in kinds:
            for name in names[kind]:
                for d in (1, -1):
                    take_z(name, d, step)

    z_round("b", 1)
    for d in (1, -1):
        take_y(0, d)
    z_round("a", 1)
    copies[("side",)].wait_recv()
    slot = period(1 - x_lo, y, core)
    for d in (1, -1):
        send(("y", 1, d), rows_ref.at[slot], rows_ref.at[slot], y_dev[d])
    twin("side", slot, 0, blocks)
    z_round("b", 2)
    for name in names["a"]:
        copies[("far", name, 1, 0)].wait_recv()
        for d in (1, -1):
            send_z(("p", name[1]), d, 1)
    z_round("a", 2)
    for d in (1, -1):
        take_y2(0, d)
    z_round("p", 1)
    z_round("b", 3)
    for d in (1, -1):
        take_y(1, d)
    z_round("a", 3)
    z_round("p", 2)
    z_round("b", 4)
    for d in (1, -1):
        take_y2(1, d)
    z_round("a", 4)
    z_round("p", 3)
    z_round("p", 4)

    taken = {("side",)}
    for key, copy in copies.items():
        copy.wait_send()
        if key[0] == "twin" or (key[0] == "far" and key[1][0] == "b"):
            copy.wait_recv()
    keep.wait()
    keep_row.wait()


def gather(ids, sens, cov, chunk=4):
    blocks, seg, cells = sens.shape
    out = jax.ShapeDtypeStruct((16, blocks, seg, cells), sens.dtype)
    copies = 200
    return pl.pallas_call(
        functools.partial(gather_kernel, chunk),
        out_shape=(out, out),
        in_specs=[
            pl.BlockSpec(memory_space=pltpu.SMEM),
            pl.BlockSpec(memory_space=pl.ANY),
            pl.BlockSpec(memory_space=pltpu.VMEM),
        ],
        out_specs=(pl.BlockSpec(memory_space=pl.ANY), pl.BlockSpec(memory_space=pl.ANY)),
        scratch_shapes=[
            pltpu.VMEM((blocks, seg, cells), sens.dtype),
            pltpu.VMEM((blocks, seg, cells), sens.dtype),
            pltpu.SemaphoreType.DMA((3,)),
            pltpu.SemaphoreType.DMA((copies,)),
            pltpu.SemaphoreType.DMA((copies,)),
        ],
        compiler_params=pltpu.CompilerParams(collective_id=1, has_side_effects=True),
        name="gather",
    )(ids, sens, cov)


NT = (((1,), (1,)), ((), ()))
WIDE = 16
NARROW = 4
GROUP = 4


def product_kernel(ids_ref, cols_hbm, rows_hbm, out_hbm, cols, rows, total, stage, count, entry, pairs, starts, in_sem, out_sem):
    row = lax.axis_index("row")
    col = lax.axis_index("col")
    stations, blocks, seg, cells = cols_hbm.shape
    groups = stations // GROUP
    per = GROUP * blocks
    model = count.shape[0]

    def load(hbm, held, n, sem):
        return pltpu.make_async_copy(hbm.at[pl.ds(n * GROUP, GROUP)], held.at[pl.ds(n * GROUP, GROUP)], in_sem.at[sem])

    for n in range(groups):
        load(cols_hbm, cols, n, n).start()
    for n in range(groups):
        load(rows_hbm, rows, n, groups + n).start()

    rows[stations] = jnp.zeros(rows.shape[1:], rows.dtype)
    total[...] = jnp.zeros_like(total)

    @pl.loop(0, model)
    def _(n):
        count[n] = 0

    @pl.loop(0, stations * blocks)
    def _(e):
        n = ids_ref[((e // blocks) * stations + col) * blocks + e % blocks]
        c = count[n]
        entry[n * stations + c] = e
        count[n] = c + 1

    def fill(g, at):
        starts[g] = at

        def one(e, at):
            n = ids_ref[row * stations * blocks + e]
            c = count[n]

            def put(i, _):
                pairs[at + i] = e * 256 + entry[n * stations + i]
                return 0

            lax.fori_loop(0, c, put, 0)
            return at + c

        at = lax.fori_loop(g * per, (g + 1) * per, one, at)
        padded = ((at + NARROW - 1) // NARROW) * NARROW

        def pad(i, _):
            pairs[i] = stations * blocks * 256
            return 0

        lax.fori_loop(at, padded, pad, 0)
        return padded

    end = lax.fori_loop(0, groups, fill, 0)
    starts[groups] = end

    def multiply(at, width):
        found = [pairs[at + i] for i in range(width)]
        left = [p // 256 for p in found]
        right = [p % 256 for p in found]
        results = [
            lax.dot_general(
                rows[e // blocks, e % blocks], cols[f // blocks, f % blocks], NT, preferred_element_type=jnp.float32
            )
            for e, f in zip(left, right)
        ]
        for e, f, r in zip(left, right, results):
            total[(e // blocks) * stations + f // blocks, :, :seg] += r

    lane = lax.broadcasted_iota(jnp.int32, (seg, 128), 1)
    for n in range(groups):
        load(cols_hbm, cols, n, n).wait()
    writes = []
    for g in range(groups):
        load(rows_hbm, rows, g, groups + g).wait()
        first = starts[g]
        size = starts[g + 1] - first
        wide = size // WIDE

        @pl.loop(0, wide)
        def _(t):
            multiply(first + t * WIDE, WIDE)

        @pl.loop(0, (size - wide * WIDE) // NARROW)
        def _(t):
            multiply(first + wide * WIDE + t * NARROW, NARROW)

        @pl.loop(g * GROUP, (g + 1) * GROUP)
        def _(b):
            for q in range(stations // 4):
                part = [total[b * stations + q * 4 + p] for p in range(4)]
                r1, r2, r3 = [pltpu.roll(part[p], 128 - 32 * p, axis=1) for p in (1, 2, 3)]
                tiles = [
                    jnp.where(lane < 96, part[0], r1),
                    jnp.where(lane < 64, r1, r2),
                    jnp.where(lane < 32, r2, r3),
                ]
                for t in range(3):
                    stage[pl.ds(b * seg * 12 + q * 3 + t, seg, stride=12), :] = tiles[t]

        chunk = GROUP * seg * 12
        write = pltpu.make_async_copy(
            stage.at[pl.ds(g * chunk, chunk)], out_hbm.at[pl.ds(g * chunk, chunk)], out_sem.at[g]
        )
        write.start()
        writes.append(write)
    for write in writes:
        write.wait()


def product(ids, cols, rows):
    stations, blocks, seg, cells = cols.shape
    lines = stations * seg * stations * seg // 128
    return pl.pallas_call(
        product_kernel,
        out_shape=jax.ShapeDtypeStruct((lines, 128), jnp.float32),
        in_specs=[
            pl.BlockSpec(memory_space=pltpu.SMEM),
            pl.BlockSpec(memory_space=pl.ANY),
            pl.BlockSpec(memory_space=pl.ANY),
        ],
        out_specs=pl.BlockSpec(memory_space=pl.ANY),
        scratch_shapes=[
            pltpu.VMEM((stations, blocks, seg, cells), cols.dtype),
            pltpu.VMEM((stations + 1, blocks, seg, cells), cols.dtype),
            pltpu.VMEM((stations * (stations + 1), seg, 128), jnp.float32),
            pltpu.VMEM((lines, 128), jnp.float32),
            pltpu.SMEM((64,), jnp.int32),
            pltpu.SMEM((64 * stations,), jnp.int32),
            pltpu.SMEM((stations * stations * blocks + 64,), jnp.int32),
            pltpu.SMEM((8,), jnp.int32),
            pltpu.SemaphoreType.DMA((8,)),
            pltpu.SemaphoreType.DMA((4,)),
        ],
        compiler_params=pltpu.CompilerParams(vmem_limit_bytes=48 * 2**20),
        name="product",
    )(ids, cols, rows)


def body(sensitivity, block_ids, covariance):
    ids = block_ids.reshape(-1)
    cols, rows = gather(ids, sensitivity[0, 0], covariance)
    lines = product(ids, cols, rows)
    stations, _, seg, _ = cols.shape
    return lines.reshape(1, stations * seg, 1, stations * seg)


def solution(mesh):
    placed = (P("row", "col", None, None, None), P(), P())
    return jax.shard_map(
        body, mesh=mesh, in_specs=placed, out_specs=P("row", None, "col", None), check_vma=False
    )
```

time: 351 us -> 86.6 us (0.25)
  waiting for transfers between devices: 152 us -> 0 us
  matrix products: 129 us -> 0 us
  Pallas kernels: 0 us -> 82.7 us
  local copies, waits for them, and re-layouts: 51.6 us -> 2.33 us
  between operations: 13.4 us -> 0.03 us
    all_gather x2 -> x0, waiting for transfers between devices: 152 us -> none  [the longest x1 117 us: body(): cols = lax.all_gather(sensitivity, 'row', axis=0, tiled=True)[:, 0]]
    dot_general x33 -> x0, matrix products: 129 us -> none  [the longest x16 74 us: one_row(): jnp.einsum('akl,alje->akje', match, cols, preferred_element_type=jnp.floa...]
    pallas_call x0 -> x2, Pallas kernels: none -> 82.7 us  [the longest x1 60.5 us: gather(): pl.pallas_call(functools.partial(gather_kernel, chunk), out_shape=(out, o...]
    dynamic_update_slice x16 -> x0, local copies, waits for them, and re-layouts: 21.8 us -> none  [tile_columns(): result = lax.map(one_row, (rows, row_ids))]
    another operation x1 -> x0, local copies, waits for them, and re-layouts: 17.2 us -> none  [body(): return tile.reshape(1, tile.shape[0], 1, tile.shape[1])]
    while x2 -> x0, local copies, waits for them, and re-layouts: 9.84 us -> none  [tile_columns(): result = lax.map(one_row, (rows, row_ids))]
  transfers between devices with their start and end apart: 2 -> 0, of which waited for: 2 -> 0; matrix products, arithmetic and copies ran while one was open for 4% -> 0% of each run, Pallas kernels for 0% -> 0%
where the time goes in v1:
time: 86.6 us; the launch traced here: 85.1 us
  Pallas kernels  82.7 us (95%)
  local copies, waits for them, and re-layouts  2.33 us (3%)
    pallas_call x1, Pallas kernels, gather(): pl.pallas_call(functools.partial(gather_kernel, chunk), out_shape=(out, o...  60.5 us
    pallas_call x1, Pallas kernels, product(): pl.pallas_call(product_kernel, out_shape=jax.ShapeDtypeStruct((lines, 128...  22.2 us

profile of v1, /device:TPU:1, one launch (start us, length us, event | category | flops | bytes accessed | tf_op | source)
XLA Modules:
  0.0 85.1 jit_solution(10387485831425552343)
XLA Ops:
  0.0 0.9 %copy.5 = s32[16,16,8]{2,1,0:T(8,128)S(1)} copy(s32[16,16,8]{1,2,0:T(8,128)} %param.4) | data formatting | bytes 16384 | tf_op args[1]
  0.9 0.7 reshape.6.ids_ref
  1.6 60.5 %gather.1 = (bf16[16,8,96,256]{3,2,1,0:T(8,128)(2,1)}, bf16[16,8,96,256]{3,2,1,0:T(8,128)(2,1)}) custom-call(s32[2048]{0:T(1024)} %reshape.6.ids_ref, bf16[8,96,256]{2,1,0:T(8,128)(2,1)} %bitcast.2, f32[64,256]{1,0:T(8,128)} %cov_ref.1), custom_call_target="tpu_custom_call" | custom-call | tf_op jit(solution)/shard_map/gather/pallas_call | solution.py:174
  62.1 0.0 copy-start
  62.2 0.7 copy-done
  62.9 22.2 %product.1 = f32[18432,128]{1,0:T(8,128)} custom-call(s32[2048]{0:T(1024)S(1)} %copy-done, bf16[16,8,96,256]{3,2,1,0:T(8,128)(2,1)} %get-tuple-element.7.cols_hbm, bf16[16,8,96,256]{3,2,1,0:T(8,128)(2,1)} %get-tuple-element.8.rows_hbm), custom_call_target="tpu_custom_call" | custom-call | tf_op jit(solution)/shard_map/product/pallas_call | solution.py:315
Async XLA Ops:
  62.1 0.7 copy-start

commit v2 on v0

v2 whole, which is shorter than its diff:
```python
import functools

import jax
import jax.numpy as jnp
from jax import lax
from jax.experimental import pallas as pl
from jax.experimental.pallas import tpu as pltpu
from jax.sharding import PartitionSpec as P

MESH = pl.DeviceIdType.MESH
NT = (((1,), (1,)), ((), ()))
NY, NZ = 4, 8
SLOTS = 4
BATCH = 16


def place():
    row = lax.axis_index("row")
    col = lax.axis_index("col")
    return row, col, row // 2, row % 2, col // 8, (col // 2) % 4, col % 2


def station(z, x_hi):
    return ((z + NZ) % NZ) * 2 + x_hi


def period(x_lo, y, core):
    return (x_lo * NY + (y + NY) % NY) * 2 + core


def row_order():
    _, _, _, _, x_lo, y, core = place()
    return [period(x, y + d, c) for x in (x_lo, 1 - x_lo) for c in (core, 1 - core) for d in (0, -1, 1, 2)]


def col_order():
    _, _, z, x_hi, _, _, _ = place()
    far = 1 - x_hi
    steps = [(0, x_hi), (-1, x_hi), (1, x_hi), (0, far), (-2, x_hi), (2, x_hi), (-1, far), (1, far)]
    steps += [(-3, x_hi), (3, x_hi), (-2, far), (2, far), (4, x_hi), (-3, far), (3, far), (4, far)]
    return [station(z + d, x) for d, x in steps]


def gather_kernel(
    ids_ref, sens_ref, cov_ref, total_hbm, cols_hbm, rows_hbm, more_ref,
    total, cols, rows, held_cols, held_rows, own, scaled, table, slots, col_at, row_at, local_sem, send_sem, recv_sem,
):
    row, col, z, x_hi, x_lo, y, core = place()
    blocks, seg, cells = sens_ref.shape
    half = blocks // 2

    z_dev = {d: (station(z + d, x_hi), col) for d in (1, -1)}
    y_dev = {d: (row, period(x_lo, y + d, core)) for d in (1, -1)}
    far_dev = (station(z, 1 - x_hi), col)
    side_dev = (row, period(1 - x_lo, y, core))
    twin_dev = (row, period(x_lo, y, 1 - core))

    load = pltpu.make_async_copy(sens_ref, own, local_sem.at[0])
    load.start()

    barrier = pltpu.get_barrier_semaphore()
    partners = [z_dev[1], z_dev[-1], y_dev[1], y_dev[-1], far_dev, side_dev, twin_dev]
    for device in partners:
        pl.semaphore_signal(barrier, inc=1, device_id=device, device_id_type=MESH)
    pl.semaphore_wait(barrier, len(partners))

    copies = {}

    def send(key, src, dst, device):
        n = len(copies)
        copy = pltpu.make_async_remote_copy(
            src_ref=src, dst_ref=dst, send_sem=send_sem.at[n], recv_sem=recv_sem.at[n], device_id=device, device_id_type=MESH
        )
        copy.start()
        copies[key] = copy

    def taken(*key):
        copies[key].wait_recv()

    def piece(kind, d, step):
        first = half if kind == "b" else 0
        if step < 4:
            return pl.ds(first, half), pl.ds(0, seg)
        return pl.ds(first, half), pl.ds(0 if d == 1 else seg // 2, seg // 2)

    def send_z(kind, d, step):
        part = piece(kind, d, step)
        slot = station(z - d * (step - 1), 1 - x_hi if kind == "p" else x_hi)
        src = sens_ref if (step == 1 and kind != "p") else cols.at[slot]
        send(("z", kind, d, step), src.at[part], cols.at[(slot, *part)], z_dev[d])

    def send_far(kind, d, step):
        part = piece(kind, d, step)
        slot = station(z - d * step, x_hi)
        src = sens_ref if step == 0 else cols.at[slot]
        send(("far", kind, d, step), src.at[part], cols.at[(slot, *part)], far_dev)

    def take_z(kind, step):
        for d in (1, -1):
            taken("z", kind, d, step)
            if step < 4:
                send_z(kind, d, step + 1)
            if kind == "b":
                send_far(kind, d, step)

    for kind in "ba":
        for d in (1, -1):
            send_z(kind, d, 1)

    load.wait()
    lane = lax.broadcasted_iota(jnp.int32, (1, 16), 1)
    model = lax.broadcasted_iota(jnp.int32, (cov_ref.shape[0], 1), 0)
    for k in range(blocks):
        mine = jnp.sum(jnp.where(lane == col, ids_ref[row, k : k + 1, :], 0), axis=1, keepdims=True)
        factor = jnp.sum(jnp.where(model == mine, cov_ref[...], 0.0), axis=0, keepdims=True)
        scaled[k] = (own[k].astype(jnp.float32) * factor).astype(jnp.bfloat16)
    send(("side",), scaled, rows.at[col], side_dev)
    for d in (1, -1):
        send(("y", 0, d), scaled, rows.at[col], y_dev[d])
    send(("twin", 0, 0), scaled, rows.at[col], twin_dev)
    send_far("a", 1, 0)
    send_far("b", 1, 0)

    def twin(line, shift, slot, first, size):
        ref = rows.at[slot, pl.ds(first, size)]
        send(("twin", line, shift), ref, ref, twin_dev)

    def take_y(line):
        for d in (1, -1):
            taken("y", line, d)
            slot = period(x_lo if line == 0 else 1 - x_lo, y - d, core)
            ref = rows.at[slot, pl.ds(0 if d == 1 else half, half)]
            send(("y2", line, d), ref, ref, y_dev[d])
            twin(line, d, slot, 0, blocks)

    def take_y2(line):
        for d in (1, -1):
            taken("y2", line, d)
            slot = period(x_lo if line == 0 else 1 - x_lo, y - 2 * d, core)
            twin(line, 2 * d, slot, 0 if d == 1 else half, half)

    def take_twin(line):
        for shift in (0, 1, -1, 2, -2):
            taken("twin", line, shift)

    at_col = lax.broadcasted_iota(jnp.int32, (16, 16), 0)
    at_row = lax.broadcasted_iota(jnp.int32, (16, 16), 1)
    other = jnp.logical_or(at_col != row, at_row != col)
    left = [jnp.broadcast_to(ids_ref[row, k : k + 1, :], (16, 16)) for k in range(blocks)]
    right = [
        jnp.broadcast_to(jnp.sum(jnp.where(at_row == col, ids_ref[:, l, :], 0), axis=1, keepdims=True), (16, 16))
        for l in range(blocks)
    ]
    count = jnp.zeros((16, 16), jnp.int32)
    found = [jnp.full((16, 16), blocks * 16, jnp.int32) for _ in range(blocks)]
    for k in range(blocks):
        for l in range(blocks):
            hit = jnp.logical_and(left[k] == right[l], other)
            for s in range(min(blocks, k + 1)):
                found[s] = jnp.where(jnp.logical_and(hit, count == s), k * 16 + l, found[s])
            count = count + hit.astype(jnp.int32)
    table[...] = jnp.zeros_like(table)
    more_ref[...] = jnp.zeros_like(more_ref)
    for s in range(SLOTS):
        table[s, :, 0:16] = found[s]
    for s in range(SLOTS, blocks):
        more_ref[s - SLOTS, :, 0:16] = found[s]
    more_ref[blocks - SLOTS, :, 0:16] = count
    more_ref[blocks - SLOTS + 1, 0:1, 0:16] = jnp.max(count, axis=0, keepdims=True)
    fill = pltpu.make_async_copy(table, slots, local_sem.at[1])
    fill.start()
    fill.wait()
    for n, (a, b) in enumerate(zip(col_order(), row_order())):
        col_at[n] = a
        row_at[n] = b

    kept = []

    def keep(src, dst):
        copy = pltpu.make_async_copy(src, dst, local_sem.at[2 + len(kept)])
        copy.start()
        kept.append(copy)

    def hold_col(n):
        slot = col_order()[n]
        src = own if n == 0 else cols.at[slot]
        keep(src, cols_hbm.at[slot])
        for k in range(blocks):
            held_cols[n * blocks + k] = src[k]

    def hold_row(n):
        slot = row_order()[n]
        src = scaled if n == 0 else rows.at[slot]
        keep(src, rows_hbm.at[slot])
        for k in range(blocks):
            held_rows[n * (blocks + 1) + k] = src[k]
        held_rows[n * (blocks + 1) + blocks] = jnp.zeros((seg, cells), jnp.bfloat16)

    def multiply(half_rows, first, last):
        @pl.loop(first, last)
        def _(n):
            a = col_at[n]
            results = []
            for m in range(8 * half_rows, 8 * half_rows + 8):
                b = row_at[m]
                codes = [slots[s, a, b] for s in range(SLOTS)]
                lhs = jnp.concatenate([held_rows[m * (blocks + 1) + (c >> 4)] for c in codes], axis=1)
                rhs = jnp.concatenate([held_cols[n * blocks + (c & 15)] for c in codes], axis=1)
                results.append(lax.dot_general(lhs, rhs, NT, preferred_element_type=jnp.float32))
            for m, result in enumerate(results):
                total[n, 8 * half_rows + m, :, 0:seg] = result

        if half_rows == 0 and first == 0:
            lhs = jnp.concatenate([scaled[k] for k in range(blocks)], axis=1)
            rhs = jnp.concatenate([own[k] for k in range(blocks)], axis=1)
            total[0, 0, :, 0:seg] = lax.dot_general(lhs, rhs, NT, preferred_element_type=jnp.float32)
        part = pl.ds(first, last - first), pl.ds(8 * half_rows, 8)
        keep(total.at[part], total_hbm.at[part])

    def take_far(step):
        for d in (1, -1):
            taken("far", "b", d, step)

    def hold_cols(*which):
        for n in which:
            hold_col(n)

    hold_row(0)
    hold_col(0)
    take_z("b", 1)
    take_y(0)
    take_z("a", 1)
    taken("side")
    slot = period(1 - x_lo, y, core)
    for d in (1, -1):
        send(("y", 1, d), rows.at[slot], rows.at[slot], y_dev[d])
    twin(1, 0, slot, 0, blocks)
    hold_cols(1, 2)
    take_z("b", 2)
    taken("far", "a", 1, 0)
    for d in (1, -1):
        send_z("p", d, 1)
    take_z("a", 2)
    take_y2(0)
    hold_cols(4, 5)
    taken("far", "b", 1, 0)
    hold_cols(3)
    for n in (1, 2, 3):
        hold_row(n)
    take_z("p", 1)
    take_twin(0)
    for n in range(4, 8):
        hold_row(n)
    multiply(0, 0, 3)
    take_z("b", 3)
    multiply(0, 3, 6)
    take_y(1)
    take_z("a", 3)
    take_far(1)
    hold_cols(6, 7)
    multiply(0, 6, 8)
    take_z("p", 2)
    take_y2(1)
    hold_cols(8, 9)
    multiply(0, 8, 10)
    take_z("b", 4)
    take_far(2)
    hold_cols(10, 11)
    multiply(0, 10, 12)
    take_twin(1)
    for n in range(8, 16):
        hold_row(n)
    multiply(1, 0, 4)
    take_z("a", 4)
    multiply(1, 4, 8)
    take_z("p", 3)
    multiply(1, 8, 12)
    hold_cols(12)
    take_far(3)
    hold_cols(13, 14)
    multiply(0, 12, 15)
    multiply(1, 12, 15)
    take_z("p", 4)
    take_far(4)
    hold_cols(15)
    multiply(0, 15, 16)
    multiply(1, 15, 16)

    for copy in copies.values():
        copy.wait_send()
    for copy in kept:
        copy.wait()


def gather(ids, sens, cov):
    blocks, seg, cells = sens.shape
    shard = (16, blocks, seg, cells)
    out = jax.ShapeDtypeStruct(shard, sens.dtype)
    copies = 64
    vmem = pl.BlockSpec(memory_space=pltpu.VMEM)
    hbm = pl.BlockSpec(memory_space=pl.ANY)
    return pl.pallas_call(
        gather_kernel,
        out_shape=(
            jax.ShapeDtypeStruct((16, 16, seg, 128), jnp.float32),
            out,
            out,
            jax.ShapeDtypeStruct((blocks - SLOTS + 2, 16, 128), jnp.int32),
        ),
        in_specs=[vmem, hbm, vmem],
        out_specs=(hbm, hbm, hbm, vmem),
        scratch_shapes=[
            pltpu.VMEM((16, 16, seg, 128), jnp.float32),
            pltpu.VMEM(shard, sens.dtype),
            pltpu.VMEM(shard, sens.dtype),
            pltpu.VMEM((16 * blocks, seg, cells), sens.dtype),
            pltpu.VMEM((16 * (blocks + 1), seg, cells), sens.dtype),
            pltpu.VMEM((blocks, seg, cells), sens.dtype),
            pltpu.VMEM((blocks, seg, cells), sens.dtype),
            pltpu.VMEM((SLOTS, 16, 128), jnp.int32),
            pltpu.SMEM((SLOTS, 16, 128), jnp.int32),
            pltpu.SMEM((16,), jnp.int32),
            pltpu.SMEM((16,), jnp.int32),
            pltpu.SemaphoreType.DMA((2 + 48,)),
            pltpu.SemaphoreType.DMA((copies,)),
            pltpu.SemaphoreType.DMA((copies,)),
        ],
        compiler_params=pltpu.CompilerParams(collective_id=1, has_side_effects=True, vmem_limit_bytes=60 * 2**20),
        name="gather",
    )(ids, sens, cov)


def product_kernel(
    total_hbm, more_hbm, cols_hbm, rows_hbm, out_hbm,
    total, stage, more, row_of, col_of, entry, left, right, more_sem, in_sem, left_sem, right_sem, out_sem,
):
    blocks, seg = cols_hbm.shape[1:3]
    tiles = 12
    fetch = pltpu.make_async_copy(more_hbm, more, more_sem.at[0])
    fetch.start()
    for n, (a, b) in enumerate(zip(col_order(), row_order())):
        col_of[a] = n
        row_of[b] = n

    def read(b):
        return pltpu.make_async_copy(total_hbm.at[:, row_of[b]], total.at[b], in_sem.at[b])

    @pl.loop(0, 16)
    def _(b):
        read(b).start()

    fetch.wait()

    def late(b):
        return more[blocks - SLOTS + 1, 0, b] > SLOTS

    def scan_row(b, n):
        def scan(a, n):
            def put(s, n):
                entry[n] = (b * 16 + a) * 256 + more[s, a, b]
                return n + 1

            return lax.fori_loop(0, jnp.maximum(more[blocks - SLOTS, a, b] - SLOTS, 0), put, n)

        return lax.fori_loop(0, jnp.where(late(b), 16, 0), scan, n)

    n_more = lax.fori_loop(0, 16, scan_row, 0)

    def blocks_of(e, i):
        code = entry[e]
        a, b, k, l = (code >> 8) & 15, code >> 12, (code >> 4) & 15, code & 15
        return (
            a,
            b,
            pltpu.make_async_copy(rows_hbm.at[b, k], left.at[i], left_sem.at[i]),
            pltpu.make_async_copy(cols_hbm.at[a, l], right.at[i], right_sem.at[i]),
        )

    def start_batch(first):
        @pl.loop(0, jnp.minimum(n_more - first, BATCH))
        def _(i):
            _, _, lhs, rhs = blocks_of(first + i, i)
            lhs.start()
            rhs.start()

    def write(b):
        chunk = seg * tiles
        part = pl.ds(pl.multiple_of(b * chunk, chunk), chunk)
        return pltpu.make_async_copy(stage.at[part], out_hbm.at[part], out_sem.at[b])

    start_batch(0)
    lane = lax.broadcasted_iota(jnp.int32, (seg, 128), 1)

    @pl.loop(0, 16)
    def _(b):
        read(b).wait()
        for q in range(4):
            part = [total[b, col_of[q * 4 + p]] for p in range(4)]
            r1, r2, r3 = [pltpu.roll(part[p], 128 - 32 * p, axis=1) for p in (1, 2, 3)]
            joined = [
                jnp.where(lane < 96, part[0], r1),
                jnp.where(lane < 64, r1, r2),
                jnp.where(lane < 32, r2, r3),
            ]
            for t in range(3):
                stage[pl.ds(b * seg * tiles + q * 3 + t, seg, stride=tiles), :] = joined[t]

        @pl.when(jnp.logical_not(late(b)))
        def _():
            write(b).start()

    @pl.when(n_more > 0)
    def _():
        @pl.loop(0, (n_more + BATCH - 1) // BATCH)
        def _(batch):
            first = batch * BATCH

            @pl.when(batch > 0)
            def _():
                start_batch(first)

            @pl.loop(0, jnp.minimum(n_more - first, BATCH))
            def _(i):
                a, b, lhs, rhs = blocks_of(first + i, i)
                lhs.wait()
                rhs.wait()
                r = lax.dot_general(left[i], right[i], NT, preferred_element_type=jnp.float32)
                r = jnp.concatenate([r, jnp.zeros((seg, 128 - seg), jnp.float32)], axis=1)
                t = a * seg // 128
                shift = a * seg % 128
                r = pltpu.roll(r, shift, axis=1)
                base = b * seg * tiles
                here = pl.ds(base + t, seg, stride=tiles)
                stage[here, :] = stage[here, :] + jnp.where(lane >= shift, r, 0.0)
                there = pl.ds(base + jnp.minimum(t + 1, tiles - 1), seg, stride=tiles)
                stage[there, :] = stage[there, :] + jnp.where(lane < shift, r, 0.0)

        @pl.loop(0, 16)
        def _(b):
            @pl.when(late(b))
            def _():
                write(b).start()

    @pl.loop(0, 16)
    def _(b):
        write(b).wait()


def product(total, more, cols, rows):
    stations, blocks, seg, cells = cols.shape
    lines = stations * seg * stations * seg // 128
    hbm = pl.BlockSpec(memory_space=pl.ANY)
    return pl.pallas_call(
        product_kernel,
        out_shape=jax.ShapeDtypeStruct((lines, 128), jnp.float32),
        in_specs=[hbm, hbm, hbm, hbm],
        out_specs=hbm,
        scratch_shapes=[
            pltpu.VMEM(total.shape, jnp.float32),
            pltpu.VMEM((lines, 128), jnp.float32),
            pltpu.SMEM(more.shape, jnp.int32),
            pltpu.SMEM((16,), jnp.int32),
            pltpu.SMEM((16,), jnp.int32),
            pltpu.SMEM((stations * stations * blocks,), jnp.int32),
            pltpu.VMEM((BATCH, seg, cells), cols.dtype),
            pltpu.VMEM((BATCH, seg, cells), cols.dtype),
            pltpu.SemaphoreType.DMA((1,)),
            pltpu.SemaphoreType.DMA((16,)),
            pltpu.SemaphoreType.DMA((BATCH,)),
            pltpu.SemaphoreType.DMA((BATCH,)),
            pltpu.SemaphoreType.DMA((16,)),
        ],
        compiler_params=pltpu.CompilerParams(vmem_limit_bytes=60 * 2**20),
        name="product",
    )(total, more, cols, rows)


def body(sensitivity, block_ids, covariance):
    ids = jnp.transpose(block_ids, (0, 2, 1))
    total, cols, rows, more = gather(ids, sensitivity[0, 0], covariance)
    lines = product(total, more, cols, rows)
    stations, _, seg, _ = cols.shape
    return lines.reshape(1, stations * seg, 1, stations * seg)


def solution(mesh):
    placed = (P("row", "col", None, None, None), P(), P())
    return jax.shard_map(
        body, mesh=mesh, in_specs=placed, out_specs=P("row", None, "col", None), check_vma=False
    )
```

time: 351 us -> 73.2 us (0.21)
  waiting for transfers between devices: 152 us -> 0 us
  matrix products: 129 us -> 0 us
  Pallas kernels: 0 us -> 73 us
  local copies, waits for them, and re-layouts: 51.6 us -> 0 us
  between operations: 13.4 us -> 0.01 us
    all_gather x2 -> x0, waiting for transfers between devices: 152 us -> none  [the longest x1 117 us: body(): cols = lax.all_gather(sensitivity, 'row', axis=0, tiled=True)[:, 0]]
    dot_general x33 -> x0, matrix products: 129 us -> none  [the longest x16 74 us: one_row(): jnp.einsum('akl,alje->akje', match, cols, preferred_element_type=jnp.floa...]
    pallas_call x0 -> x2, Pallas kernels: none -> 73 us  [the longest x1 64.4 us: gather(): pl.pallas_call(gather_kernel, out_shape=(jax.ShapeDtypeStruct((16, 16, se...]
    dynamic_update_slice x16 -> x0, local copies, waits for them, and re-layouts: 21.8 us -> none  [tile_columns(): result = lax.map(one_row, (rows, row_ids))]
    another operation x1 -> x0, local copies, waits for them, and re-layouts: 17.2 us -> none  [body(): return tile.reshape(1, tile.shape[0], 1, tile.shape[1])]
    while x2 -> x0, local copies, waits for them, and re-layouts: 9.84 us -> none  [tile_columns(): result = lax.map(one_row, (rows, row_ids))]
  transfers between devices with their start and end apart: 2 -> 0, of which waited for: 2 -> 0; matrix products, arithmetic and copies ran while one was open for 4% -> 0% of each run, Pallas kernels for 0% -> 0%
where the time goes in v2:
time: 73.2 us; the launch traced here: 73 us
  Pallas kernels  73 us (100%)
    pallas_call x1, Pallas kernels, gather(): pl.pallas_call(gather_kernel, out_shape=(jax.ShapeDtypeStruct((16, 16, se...  64.4 us
    pallas_call x1, Pallas kernels, product(): pl.pallas_call(product_kernel, out_shape=jax.ShapeDtypeStruct((lines, 128...  8.61 us

profile of v2, /device:TPU:1, one launch (start us, length us, event | category | flops | bytes accessed | tf_op | source)
XLA Modules:
  0.0 73.0 jit_solution(350807877119637640)
XLA Ops:
  0.0 64.4 %gather.1 = (f32[16,16,96,128]{3,2,1,0:T(8,128)}, bf16[16,8,96,256]{3,2,1,0:T(8,128)(2,1)}, bf16[16,8,96,256]{3,2,1,0:T(8,128)(2,1)}, s32[6,16,128]{2,1,0:T(8,128)}) custom-call(s32[16,8,16]{2,1,0:T(8,128)} %bitcast.4, bf16[8,96,256]{2,1,0:T(8,128)(2,1)} %bitcast.3, f32[64,256]{1,0:T(8,128)} %cov_ref.1), custom_call_target="tpu_custom_call" | custom-call | tf_op jit(solution)/shard_map/gather/pallas_call | solution.py:302
  64.4 8.6 %product.1 = f32[18432,128]{1,0:T(8,128)} custom-call(f32[16,16,96,128]{3,2,1,0:T(8,128)} %get-tuple-element.9.total_hbm, s32[6,16,128]{2,1,0:T(8,128)} %get-tuple-element.10.more_hbm, bf16[16,8,96,256]{3,2,1,0:T(8,128)(2,1)} %get-tuple-element.11.cols_hbm, bf16[16,8,96,256]{3,2,1,0:T(8,128)(2,1)} %get-tuple-element.12.rows_hbm), custom_call_target="tpu_custom_call" | custom-call | tf_op jit(solution)/shard_map/product/pallas_call | solution.py:453

commit v3 on v2

--- a/solution.py
+++ b/solution.py
@@ -42,8 +42,8 @@
 
 
 def gather_kernel(
-    ids_ref, sens_ref, cov_ref, total_hbm, cols_hbm, rows_hbm, more_ref,
-    total, cols, rows, held_cols, held_rows, own, scaled, table, slots, col_at, row_at, local_sem, send_sem, recv_sem,
+    ids_ref, sens_ref, cov_ref, total, cols_hbm, rows_hbm, more_hbm,
+    cols, rows, held_cols, held_rows, own, scaled, table, more, slots, col_at, row_at, local_sem, send_sem, recv_sem,
 ):
     row, col, z, x_hi, x_lo, y, core = place()
     blocks, seg, cells = sens_ref.shape
@@ -145,7 +145,6 @@
 
     at_col = lax.broadcasted_iota(jnp.int32, (16, 16), 0)
     at_row = lax.broadcasted_iota(jnp.int32, (16, 16), 1)
-    other = jnp.logical_or(at_col != row, at_row != col)
     left = [jnp.broadcast_to(ids_ref[row, k : k + 1, :], (16, 16)) for k in range(blocks)]
     right = [
         jnp.broadcast_to(jnp.sum(jnp.where(at_row == col, ids_ref[:, l, :], 0), axis=1, keepdims=True), (16, 16))
@@ -155,18 +154,19 @@
     found = [jnp.full((16, 16), blocks * 16, jnp.int32) for _ in range(blocks)]
     for k in range(blocks):
         for l in range(blocks):
-            hit = jnp.logical_and(left[k] == right[l], other)
+            hit = left[k] == right[l]
             for s in range(min(blocks, k + 1)):
                 found[s] = jnp.where(jnp.logical_and(hit, count == s), k * 16 + l, found[s])
             count = count + hit.astype(jnp.int32)
     table[...] = jnp.zeros_like(table)
-    more_ref[...] = jnp.zeros_like(more_ref)
-    for s in range(SLOTS):
+    more[...] = jnp.zeros_like(more)
+    for s in range(blocks):
         table[s, :, 0:16] = found[s]
     for s in range(SLOTS, blocks):
-        more_ref[s - SLOTS, :, 0:16] = found[s]
-    more_ref[blocks - SLOTS, :, 0:16] = count
-    more_ref[blocks - SLOTS + 1, 0:1, 0:16] = jnp.max(count, axis=0, keepdims=True)
+        more[s - SLOTS, :, 0:16] = found[s]
+    count = jnp.where(at_col == row, 0, count)
+    more[blocks - SLOTS, :, 0:16] = count
+    more[blocks - SLOTS + 1, 0:1, 0:16] = jnp.max(count, axis=0, keepdims=True)
     fill = pltpu.make_async_copy(table, slots, local_sem.at[1])
     fill.start()
     fill.wait()
@@ -196,27 +196,20 @@
             held_rows[n * (blocks + 1) + k] = src[k]
         held_rows[n * (blocks + 1) + blocks] = jnp.zeros((seg, cells), jnp.bfloat16)
 
-    def multiply(half_rows, first, last):
+    def multiply(half_rows, first, last, width=SLOTS):
         @pl.loop(first, last)
         def _(n):
             a = col_at[n]
             results = []
             for m in range(8 * half_rows, 8 * half_rows + 8):
                 b = row_at[m]
-                codes = [slots[s, a, b] for s in range(SLOTS)]
+                codes = [slots[s, a, b] for s in range(width)]
                 lhs = jnp.concatenate([held_rows[m * (blocks + 1) + (c >> 4)] for c in codes], axis=1)
                 rhs = jnp.concatenate([held_cols[n * blocks + (c & 15)] for c in codes], axis=1)
                 results.append(lax.dot_general(lhs, rhs, NT, preferred_element_type=jnp.float32))
             for m, result in enumerate(results):
                 total[n, 8 * half_rows + m, :, 0:seg] = result
 
-        if half_rows == 0 and first == 0:
-            lhs = jnp.concatenate([scaled[k] for k in range(blocks)], axis=1)
-            rhs = jnp.concatenate([own[k] for k in range(blocks)], axis=1)
-            total[0, 0, :, 0:seg] = lax.dot_general(lhs, rhs, NT, preferred_element_type=jnp.float32)
-        part = pl.ds(first, last - first), pl.ds(8 * half_rows, 8)
-        keep(total.at[part], total_hbm.at[part])
-
     def take_far(step):
         for d in (1, -1):
             taken("far", "b", d, step)
@@ -227,6 +220,7 @@
 
     hold_row(0)
     hold_col(0)
+    keep(more, more_hbm)
     take_z("b", 1)
     take_y(0)
     take_z("a", 1)
@@ -251,7 +245,8 @@
     take_twin(0)
     for n in range(4, 8):
         hold_row(n)
-    multiply(0, 0, 3)
+    multiply(0, 0, 1, blocks)
+    multiply(0, 1, 3)
     take_z("b", 3)
     multiply(0, 3, 6)
     take_y(1)
@@ -270,7 +265,8 @@
     take_twin(1)
     for n in range(8, 16):
         hold_row(n)
-    multiply(1, 0, 4)
+    multiply(1, 0, 1, blocks)
+    multiply(1, 1, 4)
     take_z("a", 4)
     multiply(1, 4, 8)
     take_z("p", 3)
@@ -295,44 +291,43 @@
 def gather(ids, sens, cov):
     blocks, seg, cells = sens.shape
     shard = (16, blocks, seg, cells)
-    out = jax.ShapeDtypeStruct(shard, sens.dtype)
     copies = 64
     vmem = pl.BlockSpec(memory_space=pltpu.VMEM)
     hbm = pl.BlockSpec(memory_space=pl.ANY)
     return pl.pallas_call(
         gather_kernel,
         out_shape=(
-            jax.ShapeDtypeStruct((16, 16, seg, 128), jnp.float32),
-            out,
-            out,
-            jax.ShapeDtypeStruct((blocks - SLOTS + 2, 16, 128), jnp.int32),
+            pltpu.VMEM((16, 16, seg, 128), jnp.float32),
+            pltpu.HBM(shard, sens.dtype),
+            pltpu.HBM(shard, sens.dtype),
+            pltpu.HBM((blocks - SLOTS + 2, 16, 128), jnp.int32),
         ),
         in_specs=[vmem, hbm, vmem],
-        out_specs=(hbm, hbm, hbm, vmem),
+        out_specs=(vmem, hbm, hbm, hbm),
         scratch_shapes=[
-            pltpu.VMEM((16, 16, seg, 128), jnp.float32),
             pltpu.VMEM(shard, sens.dtype),
             pltpu.VMEM(shard, sens.dtype),
             pltpu.VMEM((16 * blocks, seg, cells), sens.dtype),
             pltpu.VMEM((16 * (blocks + 1), seg, cells), sens.dtype),
             pltpu.VMEM((blocks, seg, cells), sens.dtype),
             pltpu.VMEM((blocks, seg, cells), sens.dtype),
-            pltpu.VMEM((SLOTS, 16, 128), jnp.int32),
-            pltpu.SMEM((SLOTS, 16, 128), jnp.int32),
+            pltpu.VMEM((blocks, 16, 128), jnp.int32),
+            pltpu.VMEM((blocks - SLOTS + 2, 16, 128), jnp.int32),
+            pltpu.SMEM((blocks, 16, 128), jnp.int32),
             pltpu.SMEM((16,), jnp.int32),
             pltpu.SMEM((16,), jnp.int32),
             pltpu.SemaphoreType.DMA((2 + 48,)),
             pltpu.SemaphoreType.DMA((copies,)),
             pltpu.SemaphoreType.DMA((copies,)),
         ],
-        compiler_params=pltpu.CompilerParams(collective_id=1, has_side_effects=True, vmem_limit_bytes=60 * 2**20),
+        compiler_params=pltpu.CompilerParams(collective_id=1, has_side_effects=True, vmem_limit_bytes=40 * 2**20),
         name="gather",
     )(ids, sens, cov)
 
 
 def product_kernel(
-    total_hbm, more_hbm, cols_hbm, rows_hbm, out_hbm,
-    total, stage, more, row_of, col_of, entry, left, right, more_sem, in_sem, left_sem, right_sem, out_sem,
+    total, more_hbm, cols_hbm, rows_hbm, out_hbm,
+    stage, more, row_of, col_of, entry, first_of, left, right, more_sem, left_sem, right_sem, out_sem,
 ):
     blocks, seg = cols_hbm.shape[1:3]
     tiles = 12
@@ -341,61 +336,12 @@
     for n, (a, b) in enumerate(zip(col_order(), row_order())):
         col_of[a] = n
         row_of[b] = n
-
-    def read(b):
-        return pltpu.make_async_copy(total_hbm.at[:, row_of[b]], total.at[b], in_sem.at[b])
-
-    @pl.loop(0, 16)
-    def _(b):
-        read(b).start()
-
-    fetch.wait()
-
-    def late(b):
-        return more[blocks - SLOTS + 1, 0, b] > SLOTS
-
-    def scan_row(b, n):
-        def scan(a, n):
-            def put(s, n):
-                entry[n] = (b * 16 + a) * 256 + more[s, a, b]
-                return n + 1
-
-            return lax.fori_loop(0, jnp.maximum(more[blocks - SLOTS, a, b] - SLOTS, 0), put, n)
-
-        return lax.fori_loop(0, jnp.where(late(b), 16, 0), scan, n)
-
-    n_more = lax.fori_loop(0, 16, scan_row, 0)
-
-    def blocks_of(e, i):
-        code = entry[e]
-        a, b, k, l = (code >> 8) & 15, code >> 12, (code >> 4) & 15, code & 15
-        return (
-            a,
-            b,
-            pltpu.make_async_copy(rows_hbm.at[b, k], left.at[i], left_sem.at[i]),
-            pltpu.make_async_copy(cols_hbm.at[a, l], right.at[i], right_sem.at[i]),
-        )
-
-    def start_batch(first):
-        @pl.loop(0, jnp.minimum(n_more - first, BATCH))
-        def _(i):
-            _, _, lhs, rhs = blocks_of(first + i, i)
-            lhs.start()
-            rhs.start()
-
-    def write(b):
-        chunk = seg * tiles
-        part = pl.ds(pl.multiple_of(b * chunk, chunk), chunk)
-        return pltpu.make_async_copy(stage.at[part], out_hbm.at[part], out_sem.at[b])
-
-    start_batch(0)
     lane = lax.broadcasted_iota(jnp.int32, (seg, 128), 1)
 
-    @pl.loop(0, 16)
-    def _(b):
-        read(b).wait()
+    def join(b):
+        m = row_of[b]
         for q in range(4):
-            part = [total[b, col_of[q * 4 + p]] for p in range(4)]
+            part = [total[col_of[q * 4 + p], m] for p in range(4)]
             r1, r2, r3 = [pltpu.roll(part[p], 128 - 32 * p, axis=1) for p in (1, 2, 3)]
             joined = [
                 jnp.where(lane < 96, part[0], r1),
@@ -405,41 +351,100 @@
             for t in range(3):
                 stage[pl.ds(b * seg * tiles + q * 3 + t, seg, stride=tiles), :] = joined[t]
 
+    def write(b):
+        chunk = seg * tiles
+        part = pl.ds(pl.multiple_of(b * chunk, chunk), chunk)
+        return pltpu.make_async_copy(stage.at[part], out_hbm.at[part], out_sem.at[b])
+
+    def late(b):
+        return more[blocks - SLOTS + 1, 0, b] > SLOTS
+
+    def scan_row(b, n):
+        first_of[b] = n
+
+        def scan(a, n):
+            def put(s, n):
+                entry[n] = (b * 16 + a) * 256 + more[s, a, b]
+                return n + 1
+
+            return lax.fori_loop(0, jnp.maximum(more[blocks - SLOTS, a, b] - SLOTS, 0), put, n)
+
+        return lax.fori_loop(0, jnp.where(late(b), 16, 0), scan, n)
+
+    def blocks_of(e):
+        code = entry[e]
+        i = e % BATCH
+        a, b, k, l = (code >> 8) & 15, code >> 12, (code >> 4) & 15, code & 15
+        return (
+            a,
+            pltpu.make_async_copy(rows_hbm.at[b, k], left.at[i], left_sem.at[i]),
+            pltpu.make_async_copy(cols_hbm.at[a, l], right.at[i], right_sem.at[i]),
+        )
+
+    def start(e):
+        _, lhs, rhs = blocks_of(e)
+        lhs.start()
+        rhs.start()
+
+    def add(b):
+        @pl.loop(first_of[b], first_of[b + 1])
+        def _(e):
+            @pl.when(e >= BATCH)
+            def _():
+                start(e)
+
+            a, lhs, rhs = blocks_of(e)
+            lhs.wait()
+            rhs.wait()
+            i = e % BATCH
+            r = lax.dot_general(left[i], right[i], NT, preferred_element_type=jnp.float32)
+            r = jnp.concatenate([r, jnp.zeros((seg, 128 - seg), jnp.float32)], axis=1)
+            t = a * seg // 128
+            shift = a * seg % 128
+            r = pltpu.roll(r, shift, axis=1)
+            base = b * seg * tiles
+            here = pl.ds(base + t, seg, stride=tiles)
+            stage[here, :] = stage[here, :] + jnp.where(lane >= shift, r, 0.0)
+            there = pl.ds(base + jnp.minimum(t + 1, tiles - 1), seg, stride=tiles)
+            stage[there, :] = stage[there, :] + jnp.where(lane < shift, r, 0.0)
+
+    pl.loop(0, 4)(join)
+    fetch.wait()
+    n_more = lax.fori_loop(0, 16, scan_row, 0)
+    first_of[16] = n_more
+    pl.loop(0, jnp.minimum(n_more, BATCH))(start)
+
+    @pl.loop(0, 4)
+    def _(b):
         @pl.when(jnp.logical_not(late(b)))
         def _():
             write(b).start()
 
-    @pl.when(n_more > 0)
-    def _():
-        @pl.loop(0, (n_more + BATCH - 1) // BATCH)
-        def _(batch):
-            first = batch * BATCH
-
-            @pl.when(batch > 0)
+    @pl.loop(4, 10)
+    def _(b):
+        join(b)
+
+        @pl.when(jnp.logical_not(late(b)))
+        def _():
+            write(b).start()
+
+    @pl.loop(0, 16)
+    def _(b):
+        @pl.when(late(b))
+        def _():
+            @pl.when(b >= 10)
             def _():
-                start_batch(first)
-
-            @pl.loop(0, jnp.minimum(n_more - first, BATCH))
-            def _(i):
-                a, b, lhs, rhs = blocks_of(first + i, i)
-                lhs.wait()
-                rhs.wait()
-                r = lax.dot_general(left[i], right[i], NT, preferred_element_type=jnp.float32)
-                r = jnp.concatenate([r, jnp.zeros((seg, 128 - seg), jnp.float32)], axis=1)
-                t = a * seg // 128
-                shift = a * seg % 128
-                r = pltpu.roll(r, shift, axis=1)
-                base = b * seg * tiles
-                here = pl.ds(base + t, seg, stride=tiles)
-                stage[here, :] = stage[here, :] + jnp.where(lane >= shift, r, 0.0)
-                there = pl.ds(base + jnp.minimum(t + 1, tiles - 1), seg, stride=tiles)
-                stage[there, :] = stage[there, :] + jnp.where(lane < shift, r, 0.0)
-
-        @pl.loop(0, 16)
-        def _(b):
-            @pl.when(late(b))
-            def _():
-                write(b).start()
+                join(b)
+
+            add(b)
+            write(b).start()
+
+    @pl.loop(10, 16)
+    def _(b):
+        @pl.when(jnp.logical_not(late(b)))
+        def _():
+            join(b)
+            write(b).start()
 
     @pl.loop(0, 16)
     def _(b):
@@ -453,31 +458,35 @@
     return pl.pallas_call(
         product_kernel,
         out_shape=jax.ShapeDtypeStruct((lines, 128), jnp.float32),
-        in_specs=[hbm, hbm, hbm, hbm],
+        in_specs=[pl.BlockSpec(memory_space=pltpu.VMEM), hbm, hbm, hbm],
         out_specs=hbm,
         scratch_shapes=[
-            pltpu.VMEM(total.shape, jnp.float32),
             pltpu.VMEM((lines, 128), jnp.float32),
             pltpu.SMEM(more.shape, jnp.int32),
             pltpu.SMEM((16,), jnp.int32),
             pltpu.SMEM((16,), jnp.int32),
             pltpu.SMEM((stations * stations * blocks,), jnp.int32),
+            pltpu.SMEM((stations + 1,), jnp.int32),
             pltpu.VMEM((BATCH, seg, cells), cols.dtype),
             pltpu.VMEM((BATCH, seg, cells), cols.dtype),
             pltpu.SemaphoreType.DMA((1,)),
-            pltpu.SemaphoreType.DMA((16,)),
             pltpu.SemaphoreType.DMA((BATCH,)),
             pltpu.SemaphoreType.DMA((BATCH,)),
             pltpu.SemaphoreType.DMA((16,)),
         ],
-        compiler_params=pltpu.CompilerParams(vmem_limit_bytes=60 * 2**20),
+        compiler_params=pltpu.CompilerParams(vmem_limit_bytes=14 * 2**20),
         name="product",
     )(total, more, cols, rows)
 
 
 def body(sensitivity, block_ids, covariance):
+    def in_hbm(x):
+        return pltpu.with_memory_space_constraint(x, pltpu.HBM)
+
     ids = jnp.transpose(block_ids, (0, 2, 1))
-    total, cols, rows, more = gather(ids, sensitivity[0, 0], covariance)
+    total, cols, rows, more = gather(in_hbm(ids), in_hbm(sensitivity[0, 0]), in_hbm(covariance))
+    total = pltpu.with_memory_space_constraint(total, pltpu.VMEM)
+    more, cols, rows = in_hbm(more), in_hbm(cols), in_hbm(rows)
     lines = product(total, more, cols, rows)
     stations, _, seg, _ = cols.shape
     return lines.reshape(1, stations * seg, 1, stations * seg)

time: 73.2 us -> 70.4 us (0.962)
  Pallas kernels: 73 us -> 70.1 us
    pallas_call x1, Pallas kernels: 8.61 us -> 6 us  [product(): pl.pallas_call(product_kernel, out_shape=jax.ShapeDtypeStruct((lines, 128...]
where the time goes in v3:
time: 70.4 us; the launch traced here: 70.2 us
  Pallas kernels  70.1 us (100%)
    pallas_call x1, Pallas kernels, gather(): pl.pallas_call(gather_kernel, out_shape=(pltpu.VMEM((16, 16, seg, 128), j...  64.1 us
    pallas_call x1, Pallas kernels, product(): pl.pallas_call(product_kernel, out_shape=jax.ShapeDtypeStruct((lines, 128...  6 us

profile of v3, /device:TPU:1, one launch (start us, length us, event | category | flops | bytes accessed | tf_op | source)
XLA Modules:
  0.0 70.2 jit_solution(2755861246648401850)
XLA Ops:
  0.0 64.1 %gather.1 = (f32[16,16,96,128]{3,2,1,0:T(8,128)S(1)}, bf16[16,8,96,256]{3,2,1,0:T(8,128)(2,1)}, bf16[16,8,96,256]{3,2,1,0:T(8,128)(2,1)}, s32[6,16,128]{2,1,0:T(8,128)}) custom-call(s32[16,8,16]{2,1,0:T(8,128)} %bitcast.4, bf16[8,96,256]{2,1,0:T(8,128)(2,1)} %bitcast.3, f32[64,256]{1,0:T(8,128)} %cov_ref.1), custom_call_target="tpu_custom_call" | custom-call | tf_op jit(solution)/shard_map/gather/pallas_call | solution.py:297
  64.2 6.0 %product.1 = f32[18432,128]{1,0:T(8,128)} custom-call(f32[16,16,96,128]{3,2,1,0:T(8,128)S(1)} %get-tuple-element.9.total, s32[6,16,128]{2,1,0:T(8,128)} %get-tuple-element.10.more_hbm, bf16[16,8,96,256]{3,2,1,0:T(8,128)(2,1)} %get-tuple-element.11.cols_hbm, bf16[16,8,96,256]{3,2,1,0:T(8,128)(2,1)} %get-tuple-element.12.rows_hbm), custom_call_target="tpu_custom_call" | custom-call | tf_op jit(solution)/shard_map/product/pallas_call | solution.py:458

commit v4 on v3

--- a/solution.py
+++ b/solution.py
@@ -42,8 +42,8 @@
 
 
 def gather_kernel(
-    ids_ref, sens_ref, cov_ref, total, cols_hbm, rows_hbm, more_hbm,
-    cols, rows, held_cols, held_rows, own, scaled, table, more, slots, col_at, row_at, local_sem, send_sem, recv_sem,
+    ids_hbm, sens_ref, cov_hbm, total, cols_hbm, rows_hbm, more_hbm,
+    ids_ref, cov_ref, cols, rows, held_cols, held_rows, own, scaled, table, more, slots, col_at, row_at, local_sem, send_sem, recv_sem,
 ):
     row, col, z, x_hi, x_lo, y, core = place()
     blocks, seg, cells = sens_ref.shape
@@ -55,13 +55,16 @@
     side_dev = (row, period(1 - x_lo, y, core))
     twin_dev = (row, period(x_lo, y, 1 - core))
 
-    load = pltpu.make_async_copy(sens_ref, own, local_sem.at[0])
-    load.start()
-
     barrier = pltpu.get_barrier_semaphore()
     partners = [z_dev[1], z_dev[-1], y_dev[1], y_dev[-1], far_dev, side_dev, twin_dev]
     for device in partners:
         pl.semaphore_signal(barrier, inc=1, device_id=device, device_id_type=MESH)
+    loads = [
+        pltpu.make_async_copy(src, dst, local_sem.at[n])
+        for n, (src, dst) in enumerate([(sens_ref, own), (ids_hbm, ids_ref), (cov_hbm, cov_ref)])
+    ]
+    for load in loads:
+        load.start()
     pl.semaphore_wait(barrier, len(partners))
 
     copies = {}
@@ -107,7 +110,8 @@
         for d in (1, -1):
             send_z(kind, d, 1)
 
-    load.wait()
+    for load in loads:
+        load.wait()
     lane = lax.broadcasted_iota(jnp.int32, (1, 16), 1)
     model = lax.broadcasted_iota(jnp.int32, (cov_ref.shape[0], 1), 0)
     for k in range(blocks):
@@ -167,7 +171,7 @@
     count = jnp.where(at_col == row, 0, count)
     more[blocks - SLOTS, :, 0:16] = count
     more[blocks - SLOTS + 1, 0:1, 0:16] = jnp.max(count, axis=0, keepdims=True)
-    fill = pltpu.make_async_copy(table, slots, local_sem.at[1])
+    fill = pltpu.make_async_copy(table, slots, local_sem.at[3])
     fill.start()
     fill.wait()
     for n, (a, b) in enumerate(zip(col_order(), row_order())):
@@ -177,7 +181,7 @@
     kept = []
 
     def keep(src, dst):
-        copy = pltpu.make_async_copy(src, dst, local_sem.at[2 + len(kept)])
+        copy = pltpu.make_async_copy(src, dst, local_sem.at[4 + len(kept)])
         copy.start()
         kept.append(copy)
 
@@ -196,19 +200,19 @@
             held_rows[n * (blocks + 1) + k] = src[k]
         held_rows[n * (blocks + 1) + blocks] = jnp.zeros((seg, cells), jnp.bfloat16)
 
-    def multiply(half_rows, first, last, width=SLOTS):
+    def multiply(row_first, row_last, first, last, width=SLOTS):
         @pl.loop(first, last)
         def _(n):
             a = col_at[n]
             results = []
-            for m in range(8 * half_rows, 8 * half_rows + 8):
+            for m in range(row_first, row_last):
                 b = row_at[m]
                 codes = [slots[s, a, b] for s in range(width)]
                 lhs = jnp.concatenate([held_rows[m * (blocks + 1) + (c >> 4)] for c in codes], axis=1)
                 rhs = jnp.concatenate([held_cols[n * blocks + (c & 15)] for c in codes], axis=1)
                 results.append(lax.dot_general(lhs, rhs, NT, preferred_element_type=jnp.float32))
-            for m, result in enumerate(results):
-                total[n, 8 * half_rows + m, :, 0:seg] = result
+            for m, result in zip(range(row_first, row_last), results):
+                total[n, m, :, 0:seg] = result
 
     def take_far(step):
         for d in (1, -1):
@@ -245,42 +249,41 @@
     take_twin(0)
     for n in range(4, 8):
         hold_row(n)
-    multiply(0, 0, 1, blocks)
-    multiply(0, 1, 3)
+    multiply(0, 8, 0, 1, blocks)
+    multiply(0, 8, 1, 3)
     take_z("b", 3)
-    multiply(0, 3, 6)
+    multiply(0, 8, 3, 6)
     take_y(1)
     take_z("a", 3)
     take_far(1)
     hold_cols(6, 7)
-    multiply(0, 6, 8)
+    multiply(0, 8, 6, 8)
     take_z("p", 2)
     take_y2(1)
     hold_cols(8, 9)
-    multiply(0, 8, 10)
+    multiply(0, 8, 8, 10)
     take_z("b", 4)
     take_far(2)
     hold_cols(10, 11)
-    multiply(0, 10, 12)
+    multiply(0, 8, 10, 12)
     take_twin(1)
     for n in range(8, 16):
         hold_row(n)
-    multiply(1, 0, 1, blocks)
-    multiply(1, 1, 4)
+    multiply(8, 16, 0, 1, blocks)
+    multiply(8, 16, 1, 4)
     take_z("a", 4)
-    multiply(1, 4, 8)
+    multiply(8, 16, 4, 8)
     take_z("p", 3)
-    multiply(1, 8, 12)
+    multiply(8, 16, 8, 12)
     hold_cols(12)
+    multiply(0, 16, 12, 13)
     take_far(3)
     hold_cols(13, 14)
-    multiply(0, 12, 15)
-    multiply(1, 12, 15)
+    multiply(0, 16, 13, 15)
     take_z("p", 4)
     take_far(4)
     hold_cols(15)
-    multiply(0, 15, 16)
-    multiply(1, 15, 16)
+    multiply(0, 16, 15, 16)
 
     for copy in copies.values():
         copy.wait_send()
@@ -302,9 +305,11 @@
             pltpu.HBM(shard, sens.dtype),
             pltpu.HBM((blocks - SLOTS + 2, 16, 128), jnp.int32),
         ),
-        in_specs=[vmem, hbm, vmem],
+        in_specs=[hbm, hbm, hbm],
         out_specs=(vmem, hbm, hbm, hbm),
         scratch_shapes=[
+            pltpu.VMEM(ids.shape, ids.dtype),
+            pltpu.VMEM(cov.shape, cov.dtype),
             pltpu.VMEM(shard, sens.dtype),
             pltpu.VMEM(shard, sens.dtype),
             pltpu.VMEM((16 * blocks, seg, cells), sens.dtype),
@@ -316,7 +321,7 @@
             pltpu.SMEM((blocks, 16, 128), jnp.int32),
             pltpu.SMEM((16,), jnp.int32),
             pltpu.SMEM((16,), jnp.int32),
-            pltpu.SemaphoreType.DMA((2 + 48,)),
+            pltpu.SemaphoreType.DMA((4 + 33,)),
             pltpu.SemaphoreType.DMA((copies,)),
             pltpu.SemaphoreType.DMA((copies,)),
         ],

time: 70.4 us -> 68.9 us (0.979)
  Pallas kernels: 70.1 us -> 68.7 us
    pallas_call x1, Pallas kernels: 64.1 us -> 62.7 us  [gather(): pl.pallas_call(gather_kernel, out_shape=(pltpu.VMEM((16, 16, seg, 128), j...]
where the time goes in v4:
time: 68.9 us; the launch traced here: 68.7 us
  Pallas kernels  68.7 us (100%)
    pallas_call x1, Pallas kernels, gather(): pl.pallas_call(gather_kernel, out_shape=(pltpu.VMEM((16, 16, seg, 128), j...  62.7 us
    pallas_call x1, Pallas kernels, product(): pl.pallas_call(product_kernel, out_shape=jax.ShapeDtypeStruct((lines, 128...  6 us

profile of v4, /device:TPU:1, one launch (start us, length us, event | category | flops | bytes accessed | tf_op | source)
XLA Modules:
  0.0 68.7 jit_solution(1542626504565473556)
XLA Ops:
  0.0 62.7 %gather.1 = (f32[16,16,96,128]{3,2,1,0:T(8,128)S(1)}, bf16[16,8,96,256]{3,2,1,0:T(8,128)(2,1)}, bf16[16,8,96,256]{3,2,1,0:T(8,128)(2,1)}, s32[6,16,128]{2,1,0:T(8,128)}) custom-call(s32[16,8,16]{2,1,0:T(8,128)} %bitcast.4, bf16[8,96,256]{2,1,0:T(8,128)(2,1)} %bitcast.3, f32[64,256]{1,0:T(8,128)} %cov_hbm.1), custom_call_target="tpu_custom_call" | custom-call | tf_op jit(solution)/shard_map/gather/pallas_call | solution.py:300
  62.7 6.0 %product.1 = f32[18432,128]{1,0:T(8,128)} custom-call(f32[16,16,96,128]{3,2,1,0:T(8,128)S(1)} %get-tuple-element.9.total, s32[6,16,128]{2,1,0:T(8,128)} %get-tuple-element.10.more_hbm, bf16[16,8,96,256]{3,2,1,0:T(8,128)(2,1)} %get-tuple-element.11.cols_hbm, bf16[16,8,96,256]{3,2,1,0:T(8,128)(2,1)} %get-tuple-element.12.rows_hbm), custom_call_target="tpu_custom_call" | custom-call | tf_op jit(solution)/shard_map/product/pallas_call | solution.py:463
